TPU v7x, 32 devices: a whole 2x2x4 slice. The times are simulated.
32 devices in a mesh: depth: 4 (over x, core), lat: 8 (over z, y).
Axes of the slice: x: 2, y: 2, z: 4, core: 2. Of those that a mesh axis runs over, the one named last changes fastest.
Arguments:
- temp_old: float32 [32, 8, 256, 128], P('depth', 'lat'), may hold values from 0 to 2.5
- material: int32 [32, 8, 256, 128], P('depth', 'lat'), may hold values from 0 to 7
- conduct_table: float32 [8], replicated, may hold values from 0.3 to 3
- capacity_table: float32 [8], replicated, may hold values from 0.5 to 2
- dyn_power: float32 [4, 8, 256, 128], P('depth', 'lat'), may hold values from 0.2 to 4
- leak_ref: float32 [4, 8, 256, 128], P('depth', 'lat'), may hold values from 0.05 to 1
- die_layer: int32 [4], replicated, may hold values from 0 to 31, as said below
Outputs:
- temp_new: float32 [32, 8, 256, 128], P('depth', 'lat')
- die_power: float32 [4, 8, 256, 128], P('depth', 'lat')
Inputs may be any that keep to these rules, and one draw needn't show every extreme that they name: `die_layer`: the 4 entries name different layers of the grid; one die lies on layer 0 and one on the top layer.
All inputs are finite; a program needn't handle non-finite values.
Results may differ from a plain program's by a relative error of at most 0.000059.
Values sent between devices are 32-bit elements; how exact they have to be, the bound alone decides.
A program may use at most 128 MiB of HBM per device.

v0:
```python
import functools

import jax
import jax.numpy as jnp
from jax import lax
from jax.experimental import pallas as pl
from jax.experimental.pallas import tpu as pltpu
from jax.sharding import PartitionSpec as P

SWEEPS = 6
COND_SLOPE = 0.15
LEAK_SLOPE = 0.5
SINK_CONDUCT = 2.0
PAD = 8
MESH = pl.DeviceIdType.MESH


def inverse(x):
    r = pl.reciprocal(x, approx=True)
    return r * (2.0 - x * r)


def harmonic(a, b):
    return 2.0 * a * b * inverse(a + b)


def lookup(table_ref, bits):
    level = [table_ref[i] for i in range(8)]
    for bit in bits:
        level = [jnp.where(bit, level[2 * i + 1], level[2 * i]) for i in range(len(level) // 2)]
    return level[0]


def kernel(
    n_lat, rows, layers,
    temp_hbm, mat_hbm, cond_tab, cap_tab, dyn_hbm, leak_hbm, die_layer,
    out_hbm, power_hbm,
    T, ZB, ZA, M, MB, MA, C, CB, CA, YS, YL, YR,
    CZM, CZP, CXM, CXP, CYM, CYP, B, DI, GX, DYN, LEAK, PS, PR, PO, PX, PW,
    zsend, zrecv, ysend, yrecv, dsend, drecv, lsem, osem,
):
    me = lax.axis_index("depth")
    lat = lax.axis_index("lat")
    top = layers - 1
    groups = rows // 8
    has_b, has_a = me > 0, me < 3
    has_l, has_r = lat > 0, lat < n_lat - 1
    sib = me + 1 - 2 * lax.rem(me, 2)
    cross = lax.rem(me + 2, 4)
    body = pl.ds(PAD, rows)
    lane = lax.broadcasted_iota(jnp.int32, (8, 128), 1)
    odd = lax.rem(lane, 2) == 1
    half = lane // 2

    zrow = jnp.zeros((PAD, 128), jnp.float32)

    def clear(z, carry):
        for s in range(SWEEPS):
            T[s, z, pl.ds(0, PAD), :] = zrow
            T[s, z, pl.ds(PAD + rows, PAD), :] = zrow
        C[z, pl.ds(0, PAD), :] = zrow
        C[z, pl.ds(PAD + rows, PAD), :] = zrow
        return carry

    lax.fori_loop(0, layers, clear, 0)

    load_t = pltpu.make_async_copy(temp_hbm, T.at[0, :, body], lsem.at[0])
    load_m = pltpu.make_async_copy(mat_hbm, M, lsem.at[1])
    load_d = pltpu.make_async_copy(dyn_hbm.at[0], DYN, lsem.at[2])
    load_l = pltpu.make_async_copy(leak_hbm.at[0], LEAK, lsem.at[3])
    load_t.start()
    load_m.start()
    load_d.start()
    load_l.start()

    barrier = pltpu.get_barrier_semaphore()

    def greet(d, l):
        pl.semaphore_signal(barrier, inc=1, device_id=(d, l), device_id_type=MESH)

    middle = jnp.logical_and(has_b, has_a)
    greet(sib, lat)
    greet(cross, lat)
    pl.when(middle)(lambda: greet(3 - me, lat))
    pl.when(has_l)(lambda: greet(me, lat - 1))
    pl.when(has_r)(lambda: greet(me, lat + 1))

    @pl.when(jnp.logical_not(has_b))
    def _():
        ZB[...] = jnp.zeros_like(ZB)
        CB[...] = jnp.zeros_like(CB)

    @pl.when(jnp.logical_not(has_a))
    def _():
        ZA[...] = jnp.zeros_like(ZA)
        CA[...] = jnp.zeros_like(CA)

    @pl.when(jnp.logical_not(has_l))
    def _():
        YL[...] = jnp.zeros_like(YL)

    @pl.when(jnp.logical_not(has_r))
    def _():
        YR[...] = jnp.zeros_like(YR)

    count = 2 + jnp.where(middle, 1, 0) + jnp.where(has_l, 1, 0) + jnp.where(has_r, 1, 0)
    pl.semaphore_wait(barrier, count)

    def remote(src, dst, ss, rs, d, l):
        return pltpu.make_async_remote_copy(
            src_ref=src, dst_ref=dst, send_sem=ss, recv_sem=rs,
            device_id=(d, l), device_id_type=MESH)

    def z_down(s):
        return remote(T.at[s, 0, body], ZA.at[s], zsend.at[s, 0], zrecv.at[s, 0], me - 1, lat)

    def z_up(s):
        return remote(T.at[s, top, body], ZB.at[s], zsend.at[s, 1], zrecv.at[s, 1], me + 1, lat)

    m_down = remote(M.at[0], MA, zsend.at[SWEEPS, 0], zrecv.at[SWEEPS, 0], me - 1, lat)
    m_up = remote(M.at[top], MB, zsend.at[SWEEPS, 1], zrecv.at[SWEEPS, 1], me + 1, lat)

    def y_part(s, g, first, size):
        part = pl.ds(first, size)
        to_left = remote(YS.at[s, part], YR.at[s, part], ysend.at[s, g, 0], yrecv.at[s, g, 0], me, lat - 1)
        to_right = remote(YS.at[s, part], YL.at[s, part], ysend.at[s, g, 1], yrecv.at[s, g, 1], me, lat + 1)
        return to_left, to_right

    def y_start(*part):
        to_left, to_right = y_part(*part)
        pl.when(has_l)(to_left.start)
        pl.when(has_r)(to_right.start)

    def y_recv(*part):
        to_left, to_right = y_part(*part)
        pl.when(has_r)(to_left.wait_recv)
        pl.when(has_l)(to_right.wait_recv)

    def y_sent(*part):
        to_left, to_right = y_part(*part)
        pl.when(has_l)(to_left.wait_send)
        pl.when(has_r)(to_right.wait_send)

    inner = layers - 2
    first_half = inner // 2
    parts = ((0, 0, 2), (1, 2, first_half), (2, 2 + first_half, inner - first_half))
    whole_part = (0, 0, layers)

    def place(z):
        return jnp.where(z == 0, 0, jnp.where(z == top, 1, z + 1))

    load_t.wait()
    pl.when(has_b)(z_down(0).start)
    pl.when(has_a)(z_up(0).start)
    my_core = lax.rem(me, 2)
    my_chip = me // 2
    base = me * layers

    def picked(die):
        at = die_layer[die] - base
        inside = jnp.logical_and(at >= 0, at < layers)
        flag = jnp.where(inside, 1.0, 0.0)
        return flag * T[0, jnp.clip(at, 0, top), body, :]

    for j in range(2):
        PS[j] = picked(1 - my_core + 2 * j)
    to_sib = remote(PS, PR, dsend.at[0], drecv.at[0], sib, lat)
    to_sib.start()
    for j in range(2):
        PO[j] = picked(my_core + 2 * j)

    load_m.wait()

    def conductivity(mat, temp):
        bits = [(mat & (1 << b)) != 0 for b in range(3)]
        return lookup(cond_tab, bits) * jnp.exp(-COND_SLOPE * temp), bits

    def cells(z, carry):
        packed_t = jnp.zeros((8, 128), jnp.float32)
        packed_c = jnp.zeros((8, 128), jnp.float32)
        for k in range(groups):
            t = T[0, z, pl.ds(PAD + 8 * k, 8), :]
            mat = M[z, pl.ds(8 * k, 8), :]
            c, bits = conductivity(mat, t)
            C[z, pl.ds(PAD + 8 * k, 8), :] = c
            DI[z, pl.ds(8 * k, 8), :] = lookup(cap_tab, bits)
            packed_t = jnp.where(half == k, pltpu.roll(t, 2 * k + 1, 1), packed_t)
            packed_c = jnp.where(half == k, pltpu.roll(c, 2 * k + 1, 1), packed_c)
        YS[0, place(z)] = packed_t
        YS[SWEEPS, place(z)] = packed_c
        return carry

    lax.fori_loop(0, layers // 2, cells, 0)

    to_sib.wait_recv()
    PX[0] = PO[1 - my_chip] + PR[1 - my_chip]
    to_cross = remote(PX.at[0], PX.at[1], dsend.at[1], drecv.at[1], cross, lat)
    to_cross.start()
    pl.when(has_b)(m_down.start)
    pl.when(has_a)(m_up.start)

    lax.fori_loop(layers // 2, layers, cells, 0)
    y_start(SWEEPS, *whole_part)
    y_start(0, *whole_part)
    load_d.wait()
    load_l.wait()

    to_cross.wait_recv()
    for k in range(groups):
        part = pl.ds(8 * k, 8)
        die_temp = PO[my_chip, part, :] + PR[my_chip, part, :] + PX[1, part, :]
        PW[me, part, :] = DYN[part, :] + LEAK[part, :] * jnp.exp(LEAK_SLOPE * die_temp)
    power_cross = remote(PW.at[me], PW.at[me], dsend.at[2], drecv.at[2], cross, lat)
    power_sib = remote(PW.at[me], PW.at[me], dsend.at[3], drecv.at[3], sib, lat)
    power_cross.start()
    power_sib.start()
    power_out = pltpu.make_async_copy(PW.at[me], power_hbm.at[0], lsem.at[4])
    power_out.start()

    @pl.when(has_b)
    def _():
        z_up(0).wait_recv()
        m_up.wait_recv()
        for k in range(groups):
            part = pl.ds(8 * k, 8)
            CB[part, :] = conductivity(MB[part, :], ZB[0, part, :])[0]

    @pl.when(has_a)
    def _():
        z_down(0).wait_recv()
        m_down.wait_recv()
        for k in range(groups):
            part = pl.ds(8 * k, 8)
            CA[part, :] = conductivity(MA[part, :], ZA[0, part, :])[0]

    y_recv(SWEEPS, *whole_part)
    y_recv(0, *whole_part)

    def halo_cols(s, z):
        p = place(z)
        return jnp.where(odd, pltpu.roll(YL[s, p], 1, 1), pltpu.roll(YR[s, p], 127, 1))

    lane0 = lane == 0
    lane_last = lane == 127

    def faces(z, below, above):
        cols = halo_cols(SWEEPS, z)
        sink = jnp.where(base + z == 0, SINK_CONDUCT, 0.0)
        for k in range(groups + 1):
            lo = C[z, pl.ds(PAD + 8 * k - 1, 8), :]
            hi = C[z, pl.ds(PAD + 8 * k, 8), :]
            GX[pl.ds(8 * k, 8), :] = 2.0 * lo * hi * inverse(jnp.maximum(lo + hi, 1e-30))
        for k in range(groups):
            part = pl.ds(8 * k, 8)
            c = C[z, pl.ds(PAD + 8 * k, 8), :]
            gzm = harmonic(c, below(k))
            gzp = harmonic(c, above(k))
            gxm = GX[part, :]
            gxp = GX[pl.ds(8 * k + 1, 8), :]
            h = pltpu.roll(cols, (127 - 2 * k) % 128, 1)
            gym = harmonic(c, jnp.where(lane0, h, pltpu.roll(c, 1, 1)))
            gyp = jnp.where(lane_last, harmonic(c, h), pltpu.roll(gym, 127, 1))
            cap = DI[z, part, :]
            inv = inverse(cap + sink + (gzm + gzp + gxm + gxp + gym + gyp))
            CZM[z, part, :] = gzm * inv
            CZP[z, part, :] = gzp * inv
            CXM[z, part, :] = gxm * inv
            CXP[z, part, :] = gxp * inv
            CYM[z, part, :] = gym * inv
            CYP[z, part, :] = gyp * inv
            DI[z, part, :] = inv
            B[z, part, :] = cap * T[0, z, pl.ds(PAD + 8 * k, 8), :] * inv

    def layer_of(ref, z):
        return lambda k: ref[z, pl.ds(PAD + 8 * k, 8), :]

    def halo_of(ref):
        return lambda k: ref[pl.ds(8 * k, 8), :]

    faces(0, halo_of(CB), layer_of(C, 1))

    def inner_faces(z, carry):
        faces(z, layer_of(C, z - 1), layer_of(C, z + 1))
        return carry

    lax.fori_loop(1, 1 + first_half, inner_faces, 0)
    power_cross.wait_recv()
    forward = remote(PW.at[cross], PW.at[cross], dsend.at[4], drecv.at[4], sib, lat)

    sib_cross = lax.rem(sib + 2, 4)
    forward.start()
    lax.fori_loop(1 + first_half, top, inner_faces, 0)
    faces(top, layer_of(C, top - 1), halo_of(CA))

    power_sib.wait_recv()
    forward.wait_recv()

    def add_source(z, carry):
        which = jnp.int32(0)
        flag = jnp.float32(0.0)
        for d in range(4):
            hit = die_layer[d] == base + z
            which = jnp.where(hit, d, which)
            flag = jnp.where(hit, 1.0, flag)
        for k in range(groups):
            part = pl.ds(8 * k, 8)
            B[z, part, :] = B[z, part, :] + flag * PW[which, part, :] * DI[z, part, :]
        return carry

    lax.fori_loop(0, layers, add_source, 0)

    def relax(s, z, below, above, last):
        cols = halo_cols(s, z)
        packed = jnp.zeros((8, 128), jnp.float32)
        for k in range(groups):
            part = pl.ds(8 * k, 8)
            at = PAD + 8 * k
            t = T[s, z, pl.ds(at, 8), :]
            h = pltpu.roll(cols, (127 - 2 * k) % 128, 1)
            left = jnp.where(lane0, h, pltpu.roll(t, 1, 1))
            right = jnp.where(lane_last, h, pltpu.roll(t, 127, 1))
            new = (B[z, part, :] + CZM[z, part, :] * below(k)) + CZP[z, part, :] * above(k)
            new += CXM[z, part, :] * T[s, z, pl.ds(at - 1, 8), :] + CXP[z, part, :] * T[s, z, pl.ds(at + 1, 8), :]
            new += CYM[z, part, :] * left + CYP[z, part, :] * right
            T[s + 1, z, pl.ds(at, 8), :] = new
            if not last:
                packed = jnp.where(half == k, pltpu.roll(new, 2 * k + 1, 1), packed)
        if not last:
            YS[s + 1, place(z)] = packed

    def out_copy(z):
        return pltpu.make_async_copy(T.at[SWEEPS, z, body], out_hbm.at[z], osem.at[z])

    def step_layers(s, last):
        def t_of(z):
            return lambda k: T[s, z, pl.ds(PAD + 8 * k, 8), :]

        def z_of(ref):
            return lambda k: ref[s, pl.ds(8 * k, 8), :]

        def inner_layer(z, carry):
            relax(s, z, t_of(z - 1), t_of(z + 1), last)
            return carry

        return t_of, z_of, inner_layer

    def sweep(s, last, first):
        t_of, z_of, inner_layer = step_layers(s, last)
        if not first:
            y_recv(s, *parts[0])
            pl.when(has_b)(z_up(s).wait_recv)
        relax(s, 0, z_of(ZB), t_of(1), last)
        if not last:
            pl.when(has_b)(z_down(s + 1).start)
        if not first:
            pl.when(has_a)(z_down(s).wait_recv)
        relax(s, top, t_of(top - 1), z_of(ZA), last)
        if not last:
            pl.when(has_a)(z_up(s + 1).start)
            y_start(s + 1, *parts[0])
        else:
            out_copy(0).start()
            out_copy(top).start()
        for g, lo, size in parts[1:]:
            if not first:
                y_recv(s, g, lo, size)
            if last:
                def with_out(z, carry):
                    inner_layer(z, carry)
                    out_copy(z).start()
                    return carry
                lax.fori_loop(lo - 1, lo - 1 + size, with_out, 0)
            else:
                lax.fori_loop(lo - 1, lo - 1 + size, inner_layer, 0)
                y_start(s + 1, g, lo, size)

    sweep(0, False, True)

    def middle_sweep(s, carry):
        sweep(s, False, False)
        return carry

    lax.fori_loop(1, SWEEPS - 1, middle_sweep, 0)
    sweep(SWEEPS - 1, True, False)

    to_sib.wait_send()
    to_cross.wait_send()
    power_cross.wait_send()
    power_sib.wait_send()
    forward.wait_send()
    pl.when(has_b)(m_down.wait_send)
    pl.when(has_a)(m_up.wait_send)
    y_sent(SWEEPS, *whole_part)
    y_sent(0, *whole_part)
    for s in range(SWEEPS):
        pl.when(has_b)(z_down(s).wait_send)
        pl.when(has_a)(z_up(s).wait_send)
        if s:
            for part in parts:
                y_sent(s, *part)
    power_out.wait()
    for z in range(layers):
        out_copy(z).wait()


def solution(mesh):
    n_lat = mesh.shape["lat"]

    def local(temp_old, material, conduct_table, capacity_table, dyn_power, leak_ref, die_layer):
        layers, _, rows, cols = temp_old.shape
        f32 = jnp.float32
        vm = pltpu.VMEM
        block = (layers, rows, cols)
        face = (rows, cols)
        dma = pltpu.SemaphoreType.DMA
        any_spec = pl.BlockSpec(memory_space=pl.ANY)
        smem = pl.BlockSpec(memory_space=pltpu.SMEM)
        temp, power = pl.pallas_call(
            functools.partial(kernel, n_lat, rows, layers),
            out_shape=(jax.ShapeDtypeStruct(block, f32), jax.ShapeDtypeStruct((1,) + face, f32)),
            in_specs=[any_spec, any_spec, smem, smem, any_spec, any_spec, smem],
            out_specs=(any_spec, any_spec),
            scratch_shapes=[
                vm((SWEEPS + 1, layers, rows + 2 * PAD, cols), f32),
                vm((SWEEPS,) + face, f32), vm((SWEEPS,) + face, f32),
                vm(block, jnp.int32), vm(face, jnp.int32), vm(face, jnp.int32),
                vm((layers, rows + 2 * PAD, cols), f32), vm(face, f32), vm(face, f32),
                vm((SWEEPS + 1, layers, 8, cols), f32),
                vm((SWEEPS + 1, layers, 8, cols), f32),
                vm((SWEEPS + 1, layers, 8, cols), f32),
            ] + [vm(block, f32)] * 8 + [
                vm((rows + 8, cols), f32),
                vm(face, f32), vm(face, f32),
                vm((2,) + face, f32), vm((2,) + face, f32), vm((2,) + face, f32), vm((2,) + face, f32),
                vm((4,) + face, f32),
                dma((SWEEPS + 1, 2)), dma((SWEEPS + 1, 2)),
                dma((SWEEPS + 1, 3, 2)), dma((SWEEPS + 1, 3, 2)),
                dma((5,)), dma((5,)), dma((5,)), dma((layers,)),
            ],
            compiler_params=pltpu.CompilerParams(
                collective_id=0, has_side_effects=True, vmem_limit_bytes=48 * 1024 * 1024),
            cost_estimate=pl.CostEstimate(flops=30_000_000, bytes_accessed=3_600_000, transcendentals=400_000),
        )(
            temp_old.reshape(block), material.reshape(block), conduct_table, capacity_table,
            dyn_power.reshape((1,) + face), leak_ref.reshape((1,) + face), die_layer)
        return temp.reshape(temp_old.shape), power.reshape(dyn_power.shape)

    lateral = P("depth", "lat", None, None)
    return jax.shard_map(
        local,
        mesh=mesh,
        in_specs=(lateral, lateral, P(), P(), lateral, lateral, P()),
        out_specs=(lateral, lateral),
        check_vma=False,
    )
```

profile of v0, /device:TPU:0, one launch (start us, length us, event | category | flops | bytes accessed | tf_op | source)
XLA Modules:
  0.0 52.5 jit_solution(916289040828232338)
XLA Ops:
  0.6 0.0 copy-start.4
  0.6 0.0 copy-start.5
  0.7 0.0 copy-start.6
  0.7 0.6 %copy-done.4 = f32[8]{0:T(128)S(1)} copy-done((f32[8]{0:T(128)S(1)}, f32[8]{0:T(128)}, u32[]{:S(2)}) %copy-start.4) | copy-done | bytes 56
  1.3 0.0 copy-done.5
  1.3 0.0 copy-done.6
  1.3 0.0 copy-start
  1.3 1.2 %copy-done = f32[8,1,256,128]{3,2,1,0:T(8,128)S(1)} copy-done((f32[8,1,256,128]{3,2,1,0:T(8,128)S(1)}, f32[8,1,256,128]{3,2,1,0:T(8,128)}, u32[]{:S(2)}) %copy-start) | copy-done | bytes 1048600
  2.5 0.0 copy-start.1
  2.5 1.2 %copy-done.1 = s32[8,1,256,128]{3,2,1,0:T(8,128)S(1)} copy-done((s32[8,1,256,128]{3,2,1,0:T(8,128)S(1)}, s32[8,1,256,128]{3,2,1,0:T(8,128)}, u32[]{:S(2)}) %copy-start.1) | copy-done | bytes 1048600
  3.8 0.0 copy-start.2
  3.8 0.9 %copy-done.2 = f32[1,1,256,128]{3,2,1,0:T(8,128)S(1)} copy-done((f32[1,1,256,128]{3,2,1,0:T(8,128)S(1)}, f32[1,1,256,128]{3,2,1,0:T(8,128)}, u32[]{:S(2)}) %copy-start.2) | copy-done | bytes 131096
  4.7 0.0 copy-start.3
  4.7 0.9 %copy-done.3 = f32[1,1,256,128]{3,2,1,0:T(8,128)S(1)} copy-done((f32[1,1,256,128]{3,2,1,0:T(8,128)S(1)}, f32[1,1,256,128]{3,2,1,0:T(8,128)}, u32[]{:S(2)}) %copy-start.3) | copy-done | bytes 131096
  5.6 45.3 %shard_map.86 = (f32[8,256,128]{2,1,0:T(8,128)S(1)}, f32[1,256,128]{2,1,0:T(8,128)S(1)}) custom-call(f32[8,256,128]{2,1,0:T(8,128)S(1)} %bitcast.8, s32[8,256,128]{2,1,0:T(8,128)S(1)} %bitcast.9, f32[8]{0:T(128)S(1)} %copy-done.4, f32[8]{0:T(128)S(1)} %copy-done.5, f32[1,256,128]{2,1,0:T(8,128)S(1)} %bitcast.11, f32[1,256,128]{2,1,0:T(8,128)S(1)} %bitcast.12, ...), custom_call_target="tpu_custom_call" | custom-call | flops 30000000 | bytes 3600000 | tf_op jit(solution)/shard_map/pallas_call | solution.py:418
  50.8 1.0 %copy.12 = f32[8,1,256,128]{3,2,1,0:T(8,128)} copy(f32[8,1,256,128]{3,2,1,0:T(8,128)S(1)} %bitcast.10) | data formatting | bytes 2097152
  51.8 0.7 %copy.13 = f32[1,1,256,128]{3,2,1,0:T(8,128)} copy(f32[1,1,256,128]{3,2,1,0:T(8,128)S(1)} %bitcast.13) | data formatting | bytes 262144
Async XLA Ops:
  0.6 0.7 %copy-start.4 = (f32[8]{0:T(128)S(1)}, f32[8]{0:T(128)}, u32[]{:S(2)}) copy-start(f32[8]{0:T(128)} %cond_tab.1) | copy-start | bytes 100
  0.6 0.7 %copy-start.5 = (f32[8]{0:T(128)S(1)}, f32[8]{0:T(128)}, u32[]{:S(2)}) copy-start(f32[8]{0:T(128)} %cap_tab.1) | copy-start | bytes 100
  0.7 0.7 %copy-start.6 = (s32[4]{0:T(128)S(1)}, s32[4]{0:T(128)}, u32[]{:S(2)}) copy-start(s32[4]{0:T(128)} %die_layer.1) | copy-start | bytes 52
  1.3 1.2 %copy-start = (f32[8,1,256,128]{3,2,1,0:T(8,128)S(1)}, f32[8,1,256,128]{3,2,1,0:T(8,128)}, u32[]{:S(2)}) copy-start(f32[8,1,256,128]{3,2,1,0:T(8,128)} %param.7) | copy-start | bytes 3145732
  2.5 1.2 %copy-start.1 = (s32[8,1,256,128]{3,2,1,0:T(8,128)S(1)}, s32[8,1,256,128]{3,2,1,0:T(8,128)}, u32[]{:S(2)}) copy-start(s32[8,1,256,128]{3,2,1,0:T(8,128)} %param.8) | copy-start | bytes 3145732
  3.8 0.9 %copy-start.2 = (f32[1,1,256,128]{3,2,1,0:T(8,128)S(1)}, f32[1,1,256,128]{3,2,1,0:T(8,128)}, u32[]{:S(2)}) copy-start(f32[1,1,256,128]{3,2,1,0:T(8,128)} %param.11) | copy-start | bytes 393220
  4.7 0.9 %copy-start.3 = (f32[1,1,256,128]{3,2,1,0:T(8,128)S(1)}, f32[1,1,256,128]{3,2,1,0:T(8,128)}, u32[]{:S(2)}) copy-start(f32[1,1,256,128]{3,2,1,0:T(8,128)} %param.12) | copy-start | bytes 393220
where the time goes:
time: 52.7 us; the launch traced here: 52.5 us
  Pallas kernels  45.3 us (86%)
  local copies, waits for them, and re-layouts  6.55 us (12%)
  between operations  0.67 us (1%)
    pallas_call x1, Pallas kernels, local(): pl.pallas_call(functools.partial(kernel, n_lat, rows, layers), out_shape=...  45.3 us
    unnamed x16, local copies, waits for them, and re-layouts  6.55 us

commit v1 on v0

--- a/solution.py
+++ b/solution.py
@@ -13,6 +13,22 @@
 SINK_CONDUCT = 2.0
 PAD = 8
 MESH = pl.DeviceIdType.MESH
+
+
+class Later:
+    def __init__(self, batch):
+        self.batch, self.held, self.rounds = batch, [], 0
+
+    def __call__(self, *stores):
+        self.held.extend(stores)
+        self.rounds += 1
+        if self.rounds % self.batch == 0:
+            self.flush()
+
+    def flush(self):
+        for ref, at, value in self.held:
+            ref[at] = value
+        self.held = []
 
 
 def inverse(x):
@@ -178,14 +194,16 @@
     def cells(z, carry):
         packed_t = jnp.zeros((8, 128), jnp.float32)
         packed_c = jnp.zeros((8, 128), jnp.float32)
+        later = Later(8)
         for k in range(groups):
             t = T[0, z, pl.ds(PAD + 8 * k, 8), :]
             mat = M[z, pl.ds(8 * k, 8), :]
             c, bits = conductivity(mat, t)
-            C[z, pl.ds(PAD + 8 * k, 8), :] = c
-            DI[z, pl.ds(8 * k, 8), :] = lookup(cap_tab, bits)
+            later((C, (z, pl.ds(PAD + 8 * k, 8), slice(None)), c),
+                  (DI, (z, pl.ds(8 * k, 8), slice(None)), lookup(cap_tab, bits)))
             packed_t = jnp.where(half == k, pltpu.roll(t, 2 * k + 1, 1), packed_t)
             packed_c = jnp.where(half == k, pltpu.roll(c, 2 * k + 1, 1), packed_c)
+        later.flush()
         YS[0, place(z)] = packed_t
         YS[SWEEPS, place(z)] = packed_c
         return carry
@@ -246,10 +264,13 @@
     def faces(z, below, above):
         cols = halo_cols(SWEEPS, z)
         sink = jnp.where(base + z == 0, SINK_CONDUCT, 0.0)
+        later = Later(8)
         for k in range(groups + 1):
             lo = C[z, pl.ds(PAD + 8 * k - 1, 8), :]
             hi = C[z, pl.ds(PAD + 8 * k, 8), :]
-            GX[pl.ds(8 * k, 8), :] = 2.0 * lo * hi * inverse(jnp.maximum(lo + hi, 1e-30))
+            later((GX, (pl.ds(8 * k, 8), slice(None)), 2.0 * lo * hi * inverse(jnp.maximum(lo + hi, 1e-30))))
+        later.flush()
+        later = Later(4)
         for k in range(groups):
             part = pl.ds(8 * k, 8)
             c = C[z, pl.ds(PAD + 8 * k, 8), :]
@@ -262,14 +283,12 @@
             gyp = jnp.where(lane_last, harmonic(c, h), pltpu.roll(gym, 127, 1))
             cap = DI[z, part, :]
             inv = inverse(cap + sink + (gzm + gzp + gxm + gxp + gym + gyp))
-            CZM[z, part, :] = gzm * inv
-            CZP[z, part, :] = gzp * inv
-            CXM[z, part, :] = gxm * inv
-            CXP[z, part, :] = gxp * inv
-            CYM[z, part, :] = gym * inv
-            CYP[z, part, :] = gyp * inv
-            DI[z, part, :] = inv
-            B[z, part, :] = cap * T[0, z, pl.ds(PAD + 8 * k, 8), :] * inv
+            at = (z, part, slice(None))
+            later(
+                (CZM, at, gzm * inv), (CZP, at, gzp * inv), (CXM, at, gxm * inv), (CXP, at, gxp * inv),
+                (CYM, at, gym * inv), (CYP, at, gyp * inv), (DI, at, inv),
+                (B, at, cap * T[0, z, pl.ds(PAD + 8 * k, 8), :] * inv))
+        later.flush()
 
     def layer_of(ref, z):
         return lambda k: ref[z, pl.ds(PAD + 8 * k, 8), :]
@@ -302,9 +321,11 @@
             hit = die_layer[d] == base + z
             which = jnp.where(hit, d, which)
             flag = jnp.where(hit, 1.0, flag)
+        later = Later(8)
         for k in range(groups):
             part = pl.ds(8 * k, 8)
-            B[z, part, :] = B[z, part, :] + flag * PW[which, part, :] * DI[z, part, :]
+            later((B, (z, part, slice(None)), B[z, part, :] + flag * PW[which, part, :] * DI[z, part, :]))
+        later.flush()
         return carry
 
     lax.fori_loop(0, layers, add_source, 0)
@@ -312,6 +333,7 @@
     def relax(s, z, below, above, last):
         cols = halo_cols(s, z)
         packed = jnp.zeros((8, 128), jnp.float32)
+        later = Later(16)
         for k in range(groups):
             part = pl.ds(8 * k, 8)
             at = PAD + 8 * k
@@ -322,9 +344,10 @@
             new = (B[z, part, :] + CZM[z, part, :] * below(k)) + CZP[z, part, :] * above(k)
             new += CXM[z, part, :] * T[s, z, pl.ds(at - 1, 8), :] + CXP[z, part, :] * T[s, z, pl.ds(at + 1, 8), :]
             new += CYM[z, part, :] * left + CYP[z, part, :] * right
-            T[s + 1, z, pl.ds(at, 8), :] = new
+            later((T, (s + 1, z, pl.ds(at, 8), slice(None)), new))
             if not last:
                 packed = jnp.where(half == k, pltpu.roll(new, 2 * k + 1, 1), packed)
+        later.flush()
         if not last:
             YS[s + 1, place(z)] = packed
 
@@ -438,7 +461,7 @@
                 dma((5,)), dma((5,)), dma((5,)), dma((layers,)),
             ],
             compiler_params=pltpu.CompilerParams(
-                collective_id=0, has_side_effects=True, vmem_limit_bytes=48 * 1024 * 1024),
+                collective_id=0, has_side_effects=True, vmem_limit_bytes=62 * 1024 * 1024),
             cost_estimate=pl.CostEstimate(flops=30_000_000, bytes_accessed=3_600_000, transcendentals=400_000),
         )(
             temp_old.reshape(block), material.reshape(block), conduct_table, capacity_table,

time: 52.7 us -> 45.3 us (0.86)
  Pallas kernels: 45.3 us -> 41.6 us
  local copies, waits for them, and re-layouts: 6.55 us -> 2.96 us
    pallas_call x1, Pallas kernels: 45.3 us -> 41.6 us  [local(): pl.pallas_call(functools.partial(kernel, n_lat, rows, layers), out_shape=...]
    unnamed x16 -> x4, local copies, waits for them, and re-layouts: 6.55 us -> 2.96 us
where the time goes in v1:
time: 45.3 us; the launch traced here: 45.2 us
  Pallas kernels  41.6 us (92%)
  local copies, waits for them, and re-layouts  2.96 us (7%)
  between operations  0.65 us (1%)
    pallas_call x1, Pallas kernels, local(): pl.pallas_call(functools.partial(kernel, n_lat, rows, layers), out_shape=...  41.6 us
    unnamed x4, local copies, waits for them, and re-layouts  2.96 us

profile of v1, /device:TPU:0, one launch (start us, length us, event | category | flops | bytes accessed | tf_op | source)
XLA Modules:
  0.0 45.2 jit_solution(17657894405129341589)
XLA Ops:
  0.6 41.6 %shard_map.86 = (f32[8,256,128]{2,1,0:T(8,128)}, f32[1,256,128]{2,1,0:T(8,128)}) custom-call(f32[8,256,128]{2,1,0:T(8,128)} %bitcast.8, s32[8,256,128]{2,1,0:T(8,128)} %bitcast.9, f32[8]{0:T(128)} %cond_tab.1, f32[8]{0:T(128)} %cap_tab.1, f32[1,256,128]{2,1,0:T(8,128)} %bitcast.11, f32[1,256,128]{2,1,0:T(8,128)} %bitcast.12, s32[4]{0:T(128)} %die_layer.1), custom_call_target="tpu_custom_call" | custom-call | flops 30000000 | bytes 3600000 | tf_op jit(solution)/shard_map/pallas_call | solution.py:441
  42.2 0.0 copy-start
  42.2 2.3 %copy.12 = f32[8,1,256,128]{3,2,1,0:T(8,128)} copy(f32[8,1,256,128]{3,2,1,0:T(8,128)} %bitcast.10) | data formatting | bytes 2097152
  44.5 0.0 copy-done
  44.5 0.7 %copy.13 = f32[1,1,256,128]{3,2,1,0:T(8,128)} copy(f32[1,1,256,128]{3,2,1,0:T(8,128)S(1)} %bitcast.13) | data formatting | bytes 262144
Async XLA Ops:
  42.2 2.3 %copy-start = (f32[1,256,128]{2,1,0:T(8,128)S(1)}, f32[1,256,128]{2,1,0:T(8,128)}, u32[]{:S(2)}) copy-start(f32[1,256,128]{2,1,0:T(8,128)} %get-tuple-element.5) | copy-start | bytes 393220

commit v2 on v1

--- a/solution.py
+++ b/solution.py
@@ -274,7 +274,7 @@
         for k in range(groups):
             part = pl.ds(8 * k, 8)
             c = C[z, pl.ds(PAD + 8 * k, 8), :]
-            gzm = harmonic(c, below(k))
+            gzm = below(k)
             gzp = harmonic(c, above(k))
             gxm = GX[part, :]
             gxp = GX[pl.ds(8 * k + 1, 8), :]
@@ -286,7 +286,7 @@
             at = (z, part, slice(None))
             later(
                 (CZM, at, gzm * inv), (CZP, at, gzp * inv), (CXM, at, gxm * inv), (CXP, at, gxp * inv),
-                (CYM, at, gym * inv), (CYP, at, gyp * inv), (DI, at, inv),
+                (CB, (part, slice(None)), gzp), (CYM, at, gym * inv), (CYP, at, gyp * inv), (DI, at, inv),
                 (B, at, cap * T[0, z, pl.ds(PAD + 8 * k, 8), :] * inv))
         later.flush()
 
@@ -296,10 +296,10 @@
     def halo_of(ref):
         return lambda k: ref[pl.ds(8 * k, 8), :]
 
-    faces(0, halo_of(CB), layer_of(C, 1))
+    faces(0, lambda k: harmonic(C[0, pl.ds(PAD + 8 * k, 8), :], CB[pl.ds(8 * k, 8), :]), layer_of(C, 1))
 
     def inner_faces(z, carry):
-        faces(z, layer_of(C, z - 1), layer_of(C, z + 1))
+        faces(z, halo_of(CB), layer_of(C, z + 1))
         return carry
 
     lax.fori_loop(1, 1 + first_half, inner_faces, 0)
@@ -309,7 +309,7 @@
     sib_cross = lax.rem(sib + 2, 4)
     forward.start()
     lax.fori_loop(1 + first_half, top, inner_faces, 0)
-    faces(top, layer_of(C, top - 1), halo_of(CA))
+    faces(top, halo_of(CB), halo_of(CA))
 
     power_sib.wait_recv()
     forward.wait_recv()

time: 45.3 us -> 45.3 us (level)
  no operation moved by 1% of the time
where the time goes in v2:
time: 45.3 us; the launch traced here: 45.1 us
  Pallas kernels  41.5 us (92%)
  local copies, waits for them, and re-layouts  2.96 us (7%)
  between operations  0.65 us (1%)
    pallas_call x1, Pallas kernels, local(): pl.pallas_call(functools.partial(kernel, n_lat, rows, layers), out_shape=...  41.5 us
    unnamed x4, local copies, waits for them, and re-layouts  2.96 us

profile of v2, /device:TPU:0, one launch (start us, length us, event | category | flops | bytes accessed | tf_op | source)
XLA Modules:
  0.0 45.1 jit_solution(9103615260897412805)
XLA Ops:
  0.6 41.5 %shard_map.86 = (f32[8,256,128]{2,1,0:T(8,128)}, f32[1,256,128]{2,1,0:T(8,128)}) custom-call(f32[8,256,128]{2,1,0:T(8,128)} %bitcast.8, s32[8,256,128]{2,1,0:T(8,128)} %bitcast.9, f32[8]{0:T(128)} %cond_tab.1, f32[8]{0:T(128)} %cap_tab.1, f32[1,256,128]{2,1,0:T(8,128)} %bitcast.11, f32[1,256,128]{2,1,0:T(8,128)} %bitcast.12, s32[4]{0:T(128)} %die_layer.1), custom_call_target="tpu_custom_call" | custom-call | flops 30000000 | bytes 3600000 | tf_op jit(solution)/shard_map/pallas_call | solution.py:441
  42.1 0.0 copy-start
  42.1 2.3 %copy.12 = f32[8,1,256,128]{3,2,1,0:T(8,128)} copy(f32[8,1,256,128]{3,2,1,0:T(8,128)} %bitcast.10) | data formatting | bytes 2097152
  44.4 0.0 copy-done
  44.4 0.7 %copy.13 = f32[1,1,256,128]{3,2,1,0:T(8,128)} copy(f32[1,1,256,128]{3,2,1,0:T(8,128)S(1)} %bitcast.13) | data formatting | bytes 262144
Async XLA Ops:
  42.1 2.3 %copy-start = (f32[1,256,128]{2,1,0:T(8,128)S(1)}, f32[1,256,128]{2,1,0:T(8,128)}, u32[]{:S(2)}) copy-start(f32[1,256,128]{2,1,0:T(8,128)} %get-tuple-element.5) | copy-start | bytes 393220
